TPU v7x, 256 devices: a whole 4x4x8 slice. The times are simulated.
256 devices in a mesh: lat: 32 (over x_hi, z, core), ch: 8 (over y, x_lo).
Axes of the slice: x: 4 (x_hi: 2, x_lo: 2; x = x_hi * 2 + x_lo), y: 4, z: 8, core: 2. Of those that a mesh axis runs over, the one named last changes fastest.
Arguments:
- fields: bfloat16 [768, 224, 384], P('ch', 'lat'), may hold values from -60 to 60
- gain_first: float32 [768], P('ch'), may hold values from 0.5 to 1.5
- w_inner: float32 [2, 8, 96, 96], P(None, 'ch'), may hold values from -0.4375 to 0.4375
- w_outer: float32 [2, 8, 96, 96], P(None, 'ch'), may hold values from -0.4375 to 0.4375
- gain_second: float32 [768], P('ch'), may hold values from 0.5 to 1.5
- fc_in: bfloat16 [768, 3072], P(None, 'ch'), may hold values from -0.21875 to 0.21875
- fc_out: bfloat16 [3072, 768], P('ch'), may hold values from -0.109375 to 0.109375
- cotangent: bfloat16 [768, 224, 384], P('ch', 'lat'), may hold values from -40 to 40
Outputs:
- output: bfloat16 [768, 224, 384], P('ch', 'lat')
- grad_fields: bfloat16 [768, 224, 384], P('ch', 'lat')
- grad_gain_first: float32 [768], P('ch')
- grad_w_inner: float32 [2, 8, 96, 96], P(None, 'ch')
- grad_w_outer: float32 [2, 8, 96, 96], P(None, 'ch')
- grad_gain_second: float32 [768], P('ch')
- grad_fc_in: float32 [768, 3072], P(None, 'ch')
- grad_fc_out: float32 [3072, 768], P('ch')
All inputs are finite; a program needn't handle non-finite values.
Results may differ from a plain program's by a relative error of at most 0.0056.
Values may be sent and summed in bfloat16 or wider, within the bound.
No kernel may reach another device: no remote copies, remote signals or barrier semaphores. Data moves between devices by JAX's collectives and lax.ppermute only.
A program may use at most 128 MiB of HBM per device.

v0:
```python
import math

import jax
import jax.numpy as jnp
from jax import lax
from jax.sharding import PartitionSpec as P

BS = 96
KW = 192
C = 768


EPSILON = 1e-05
HIGHEST = lax.Precision.HIGHEST
CONTRACT_LEAD = (((0,), (0,)), ((), ()))
CONTRACT_LAST = (((1,), (1,)), ((), ()))


def gelu_value(values):
    return 0.5 * values * (1.0 + lax.erf(values * 0.7071067811865476))


def gelu_slope(values):
    return 0.5 * (
        1.0 + lax.erf(values * 0.7071067811865476)
    ) + values * 0.3989422804014327 * jnp.exp(-0.5 * values * values)


def normalize(values):
    total_sum, total_squares = lax.psum((jnp.sum(values, 0), jnp.sum(values * values, 0)), "ch")
    average = total_sum / C
    inv_std = lax.rsqrt(total_squares / C - average * average + EPSILON)
    return ((values - average) * inv_std, inv_std)


def norm_back(gradient, normed, inv_std):
    leading, paired = lax.psum((jnp.sum(gradient, 0), jnp.sum(gradient * normed, 0)), "ch")
    return inv_std * (gradient - leading / C - normed * (paired / C))


def phases(first_len, second_len, length):
    product = (
        jnp.arange(first_len, dtype=jnp.int32)[:, None]
        * jnp.arange(second_len, dtype=jnp.int32)[None, :]
        % length
    )
    return product.astype(jnp.float32) * (2.0 * math.pi / length)


def lat_tables(full_rows):
    angles = phases(full_rows, full_rows, full_rows)
    factor = 1.0 / math.sqrt(full_rows)
    return (jnp.cos(angles) * factor, jnp.sin(angles) * factor)


def matmul_high(left, right):
    return jnp.matmul(left, right, precision=HIGHEST)


def to_modes(grid_field, mode_weight, full_rows):
    lon_cells = grid_field.shape[2]
    angles = phases(lon_cells, KW, lon_cells)
    dft_table = jnp.stack([jnp.cos(angles), -jnp.sin(angles)]) * (
        mode_weight / math.sqrt(lon_cells)
    )
    spectrum = jnp.einsum("clw,rwk->crkl", grid_field, dft_table, precision=HIGHEST)
    lat_cos, lat_sin = lat_tables(full_rows)
    portion = lax.all_to_all(spectrum, "lat", split_axis=2, concat_axis=3, tiled=True)
    real_part = portion[:, 0]
    imag_part = portion[:, 1]
    new_real = matmul_high(real_part, lat_cos) + matmul_high(imag_part, lat_sin)
    new_imag = matmul_high(imag_part, lat_cos) - matmul_high(real_part, lat_sin)
    return jnp.stack([new_real, new_imag], 1)


def to_grid(spectrum, mode_weight, lon_cells):
    lat_cos, lat_sin = lat_tables(spectrum.shape[3])
    real_part = spectrum[:, 0]
    imag_part = spectrum[:, 1]
    new_real = matmul_high(real_part, lat_cos) - matmul_high(imag_part, lat_sin)
    new_imag = matmul_high(imag_part, lat_cos) + matmul_high(real_part, lat_sin)
    rotated = jnp.stack([new_real, new_imag], 1)
    angles = phases(KW, lon_cells, lon_cells)
    dft_table = jnp.stack([jnp.cos(angles), -jnp.sin(angles)]) * (
        mode_weight[:, None] / math.sqrt(lon_cells)
    )
    return jnp.einsum(
        "crkl,rkw->clw",
        lax.all_to_all(rotated, "lat", split_axis=3, concat_axis=2, tiled=True),
        dft_table,
        precision=HIGHEST,
    )


def as_blocks(spectrum):
    return spectrum.reshape(spectrum.shape[0] // BS, BS, 2, spectrum.shape[2] * spectrum.shape[3])


def block_apply(matrix, operand, pattern):
    return jnp.einsum(pattern, matrix, operand, precision=HIGHEST)


def complex_apply(weight, operand):
    pattern = "bij,bjm->bim"
    real_part = operand[:, :, 0]
    imag_part = operand[:, :, 1]
    new_real = block_apply(weight[0], real_part, pattern) - block_apply(
        weight[1], imag_part, pattern
    )
    new_imag = block_apply(weight[0], imag_part, pattern) + block_apply(
        weight[1], real_part, pattern
    )
    return jnp.stack([new_real, new_imag], 2)


def complex_back(weight, gradient):
    pattern = "bji,bjm->bim"
    real_part = gradient[:, :, 0]
    imag_part = gradient[:, :, 1]
    new_real = block_apply(weight[0], real_part, pattern) + block_apply(
        weight[1], imag_part, pattern
    )
    new_imag = block_apply(weight[0], imag_part, pattern) - block_apply(
        weight[1], real_part, pattern
    )
    return jnp.stack([new_real, new_imag], 2)


def complex_weight_grad(gradient, operand):
    pattern = "bim,bjm->bij"
    grad_real = gradient[:, :, 0]
    grad_imag = gradient[:, :, 1]
    operand_real = operand[:, :, 0]
    operand_imag = operand[:, :, 1]
    weight_real = block_apply(grad_real, operand_real, pattern) + block_apply(
        grad_imag, operand_imag, pattern
    )
    weight_imag = block_apply(grad_imag, operand_real, pattern) - block_apply(
        grad_real, operand_imag, pattern
    )
    return jnp.stack([weight_real, weight_imag], 0)


def body(fields, gain_first, w_inner, w_outer, gain_second, fc_in, fc_out, cotangent):
    channels, lat_rows, lon_cells = fields.shape
    full_rows = lat_rows * lax.axis_size("lat")
    tokens = lat_rows * lon_cells
    mode_index = jnp.arange(KW, dtype=jnp.int32)
    doubled = jnp.where(mode_index == 0, 1.0, 2.0).astype(jnp.float32)
    single = jnp.ones((KW,), jnp.float32)
    mode_shape = (channels, 2, KW // lax.axis_size("lat"), full_rows)
    x_float = fields.astype(jnp.float32)
    normed_in, inv_std_in = normalize(x_float)
    lifted = normed_in * gain_first[:, None, None]
    spectrum = as_blocks(to_modes(lifted, single, full_rows))
    pre_modes = complex_apply(w_inner, spectrum)
    act_modes = gelu_value(pre_modes)
    out_modes = complex_apply(w_outer, act_modes)
    filtered = to_grid(out_modes.reshape(mode_shape), doubled, lon_cells)
    mixed_in = filtered + lifted + x_float
    normed_mid, inv_std_mid = normalize(mixed_in)
    mlp_input = (
        (normed_mid * gain_second[:, None, None]).astype(jnp.bfloat16).reshape(channels, tokens)
    )
    inputs_full = lax.all_gather(mlp_input, "ch", axis=0, tiled=True)
    pre_act = lax.dot_general(fc_in, inputs_full, CONTRACT_LEAD, preferred_element_type=jnp.float32)
    hidden = gelu_value(pre_act).astype(jnp.bfloat16)
    mixed_out = lax.psum_scatter(
        lax.dot_general(fc_out, hidden, CONTRACT_LEAD, preferred_element_type=jnp.float32).astype(
            jnp.bfloat16
        ),
        "ch",
        scatter_dimension=0,
        tiled=True,
    ).astype(jnp.float32)
    output = (
        (mixed_in.reshape(channels, tokens) + mixed_out).astype(jnp.bfloat16).reshape(fields.shape)
    )
    grad_rows = cotangent.reshape(channels, tokens)
    grad_full = lax.all_gather(grad_rows, "ch", axis=0, tiled=True)
    grad_hidden = jnp.dot(fc_out, grad_full, preferred_element_type=jnp.float32)
    grad_pre = (grad_hidden * gelu_slope(pre_act)).astype(jnp.bfloat16)
    grad_fc_out = lax.dot_general(
        hidden, grad_full, CONTRACT_LAST, preferred_element_type=jnp.float32
    )
    grad_fc_in = lax.dot_general(
        inputs_full, grad_pre, CONTRACT_LAST, preferred_element_type=jnp.float32
    )
    grad_input = lax.psum_scatter(
        jnp.dot(fc_in, grad_pre, preferred_element_type=jnp.float32),
        "ch",
        scatter_dimension=0,
        tiled=True,
    )
    normed_rows = normed_mid.reshape(channels, tokens)
    grad_gain_second = jnp.sum(grad_input * normed_rows, 1)
    grad_mixed = grad_rows.astype(jnp.float32) + norm_back(
        grad_input * gain_second[:, None], normed_rows, inv_std_mid.reshape(tokens)
    )
    grad_mixed = grad_mixed.reshape(fields.shape)
    grad_modes = as_blocks(to_modes(grad_mixed, doubled, full_rows))
    grad_act = complex_back(w_outer, grad_modes)
    grad_w_outer = complex_weight_grad(grad_modes, act_modes)
    grad_pre_modes = grad_act * gelu_slope(pre_modes)
    grad_w_inner = complex_weight_grad(grad_pre_modes, spectrum)
    grad_spectrum = complex_back(w_inner, grad_pre_modes)
    grad_lifted = to_grid(grad_spectrum.reshape(mode_shape), single, lon_cells) + grad_mixed
    grad_gain_first = jnp.sum(grad_lifted * normed_in, (1, 2))
    grad_fields = (
        grad_mixed + norm_back(grad_lifted * gain_first[:, None, None], normed_in, inv_std_in)
    ).astype(jnp.bfloat16)
    grad_fc_in, grad_fc_out, grad_gain_second, grad_w_inner, grad_w_outer, grad_gain_first = (
        lax.psum(
            (
                grad_fc_in,
                grad_fc_out,
                grad_gain_second,
                grad_w_inner,
                grad_w_outer,
                grad_gain_first,
            ),
            "lat",
        )
    )
    return (
        output,
        grad_fields,
        grad_gain_first,
        grad_w_inner,
        grad_w_outer,
        grad_gain_second,
        grad_fc_in,
        grad_fc_out,
    )


def solution(mesh):
    placed = (
        P("ch", "lat", None),
        P("ch"),
        P(None, "ch", None, None),
        P(None, "ch", None, None),
        P("ch"),
        P(None, "ch"),
        P("ch", None),
        P("ch", "lat", None),
    )
    return jax.shard_map(
        body,
        mesh=mesh,
        in_specs=placed,
        out_specs=(
            P("ch", "lat", None),
            P("ch", "lat", None),
            P("ch"),
            P(None, "ch", None, None),
            P(None, "ch", None, None),
            P("ch"),
            P(None, "ch"),
            P("ch", None),
        ),
        check_vma=False,
    )
```

profile of v0, /device:TPU:8, one launch (start us, length us, event | category | flops | bytes accessed | tf_op | source)
XLA Modules:
  0.0 1056.3 jit_solution(8026631989302953367)
XLA Ops:
  9.9 32.3 %all-reduce.5 = (f32[7,384]{1,0:T(8,128)S(1)}, f32[7,384]{1,0:T(8,128)S(1)}) all-reduce(f32[7,384]{1,0:T(8,128)S(1)} %get-tuple-element.57, f32[7,384]{1,0:T(8,128)S(1)} %get-tuple-element.56), channel_id=1, replica_groups=mesh['lat'=32,'ch'=8] {'ch'}, use_global_device_ids=true, to_apply=%region_3.4 | all-reduce | flops 5376 | bytes 43008 | tf_op jit(solution)/shard_map/psum | solution.py:30
  42.2 3.4 convolution_bitcast_fusion.3
  46.7 49.3 %all_to_all.72 = f32[96,2,192,7]{0,1,3,2:T(2,128)S(1)} all-to-all(f32[96,2,192,7]{0,1,3,2:T(2,128)S(1)} %copy.155), channel_id=1, replica_groups=mesh['lat'=32,'ch'=8] {'lat'}, dimensions={2} | all-to-all | bytes 2064384 | tf_op jit(solution)/shard_map/all_to_all | solution.py:68
  97.7 2.0 fusion.125
  99.7 2.0 fusion.127
  101.7 2.8 convolution_subtract_fusion.5
  104.5 2.0 convolution_add_fusion.5
  118.3 2.5 fusion.7
  120.8 2.3 squeeze.18
  123.1 2.7 fusion.81
  131.9 3.4 copy.165
  135.4 4.7 all-to-all-start.1
  141.4 35.2 %all-to-all-done.1 = f32[96,2,6,224]{0,1,2,3:T(2,128)} async-done(((f32[96,2,6,224]{0,1,2,3:T(2,128)}), f32[96,2,6,224]{0,1,2,3:T(2,128)}, u32[]{:S(2)}, u32[]{:S(2)}) %all-to-all-start.1) | async-done | bytes 1032224 | tf_op jit(solution)/shard_map/all_to_all | solution.py:89
  178.4 3.8 fusion.303
  182.2 30.9 %all-reduce.4 = (f32[7,384]{1,0:T(8,128)S(1)}, f32[7,384]{1,0:T(8,128)S(1)}) all-reduce(f32[7,384]{1,0:T(8,128)S(1)} %get-tuple-element.55, f32[7,384]{1,0:T(8,128)S(1)} %get-tuple-element.54), channel_id=1, replica_groups=mesh['lat'=32,'ch'=8] {'ch'}, use_global_device_ids=true, to_apply=%region_7.8 | all-reduce | flops 5376 | bytes 43008 | tf_op jit(solution)/shard_map/psum | solution.py:30
  213.1 2.4 fusion.57
  217.6 85.6 %all-gather.3.cloned.1.call-done = bf16[768,2688]{1,0:T(8,128)(2,1)} async-done(((bf16[96,2688]{1,0:T(8,128)(2,1)}), bf16[768,2688]{1,0:T(8,128)(2,1)}) %all-gather.3.cloned.1.call-update) | async-done | bytes 4128784 | tf_op jit(solution)/shard_map/all_gather | solution.py:165
  303.2 8.0 multiply_convert_fusion
  311.2 86.4 %all-gather.5.cloned.1.call-done = bf16[768,2688]{1,0:T(8,128)(2,1)} async-done(((bf16[96,2688]{1,0:T(8,128)(2,1)}), bf16[768,2688]{1,0:T(8,128)(2,1)}) %all-gather.5.cloned.1.call-update) | async-done | bytes 4128784 | tf_op jit(solution)/shard_map/all_gather | solution.py:180
  397.6 8.2 fusion.1
  407.1 5.6 convolution_bitcast_fusion
  412.7 8.9 copy.204
  422.9 169.1 %reduce-scatter.9.cloned.1.call-done = f32[96,2688]{1,0:T(8,128)} async-done(((f32[768,2688]{1,0:T(8,128)}), f32[96,2688]{1,0:T(8,128)}) %reduce-scatter.9.cloned.1.call-update) | async-done | bytes 1032208 | tf_op jit(solution)/shard_map/reduce_scatter | solution.py:189
  592.0 2.1 multiply_reduce_fusion
  594.1 30.9 %all-reduce.3 = (f32[2688]{0:T(1024)S(1)}, f32[2688]{0:T(1024)S(1)}) all-reduce(f32[2688]{0:T(1024)S(1)} %get-tuple-element.49, f32[2688]{0:T(1024)S(1)} %get-tuple-element.53), channel_id=1, replica_groups=mesh['lat'=32,'ch'=8] {'ch'}, use_global_device_ids=true, to_apply=%region_13.14 | all-reduce | flops 5376 | bytes 43008 | tf_op jit(solution)/shard_map/psum | solution.py:37
  627.6 2.6 convolution_bitcast_fusion.2
  630.3 2.1 copy.177
  632.4 10.3 all-to-all-start.2
  642.8 5.9 fusion
  648.7 6.5 copy.202
  655.2 5.9 fusion.307
  661.1 3.3 fusion.306
  664.5 14.8 %all-to-all-done.2 = f32[96,2,192,7]{0,1,3,2:T(2,128)} async-done(((f32[96,2,192,7]{0,1,3,2:T(2,128)}), f32[96,2,192,7]{0,1,3,2:T(2,128)}, u32[]{:S(2)}, u32[]{:S(2)}) %all-to-all-start.2) | async-done | bytes 1032224 | tf_op jit(solution)/shard_map/all_to_all | solution.py:68
  682.1 2.0 fusion.121
  684.1 2.0 convolution_add_fusion.4
  688.9 3.3 fusion.119
  692.2 2.4 convolution_subtract_fusion.4
  702.6 2.3 squeeze.23
  707.0 2.3 squeeze.22
  709.4 2.8 fusion.75
  718.5 3.4 copy.187
  721.9 4.7 all-to-all-start.3
  734.4 30.1 %reduce-scatter.7.cloned.1.call-done = bf16[96,2688]{1,0:T(8,128)(2,1)} async-done(((bf16[768,2688]{1,0:T(8,128)(2,1)}), bf16[96,2688]{1,0:T(8,128)(2,1)}) %reduce-scatter.7.cloned.1.call-update) | async-done | bytes 516112 | tf_op jit(solution)/shard_map/reduce_scatter | solution.py:168
  768.5 2.8 fusion.55
  771.3 69.8 %all-reduce = (f32[96]{0:T(128)}, f32[96]{0:T(128)}) all-reduce(f32[96]{0:T(128)S(1)} %get-tuple-element.50, f32[96]{0:T(128)S(1)} %copy-done.43), channel_id=1, replica_groups=mesh['lat'=32,'ch'=8] {'lat'}, use_global_device_ids=true, to_apply=%region_19.20 | all-reduce | flops 192 | bytes 1536 | tf_op jit(solution)/shard_map/psum | solution.py:213
  841.1 33.1 %all-reduce.2 = (f32[7,384]{1,0:T(8,128)S(1)}, f32[7,384]{1,0:T(8,128)S(1)}) all-reduce(f32[7,384]{1,0:T(8,128)S(1)} %get-tuple-element.51, f32[7,384]{1,0:T(8,128)S(1)} %get-tuple-element.52), channel_id=1, replica_groups=mesh['lat'=32,'ch'=8] {'ch'}, use_global_device_ids=true, to_apply=%region_17.18 | all-reduce | flops 5376 | bytes 43008 | tf_op jit(solution)/shard_map/psum | solution.py:37
  875.4 167.6 %all-reduce.8.cloned.1.call-done = (f32[2,1,96,96]{3,2,1,0:T(8,128)}, f32[2,1,96,96]{3,2,1,0:T(8,128)}, f32[768,384]{1,0:T(8,128)}, f32[384,768]{1,0:T(8,128)}) async-done(((f32[2,1,96,96]{3,2,1,0:T(8,128)}, f32[2,1,96,96]{3,2,1,0:T(8,128)}, f32[768,384]{1,0:T(8,128)}, f32[384,768]{1,0:T(8,128)}), (f32[2,1,96,96]{3,2,1,0:T(8,128)}, f32[2,1,96,96]{3,2,1,0:T(8,128)}, f32[768,384]{1,0:T(8,128)}, ...) | async-done | bytes 2506768 | tf_op jit(solution)/shard_map/psum | solution.py:213
  1046.2 2.4 copy.264
  (178 shorter events, 72.2 us)
Async XLA Ops:
  7.2 296.0 %copy-start = (bf16[768,384]{1,0:T(8,128)(2,1)S(1)}, bf16[768,384]{1,0:T(8,128)(2,1)}, u32[]{:S(2)}) copy-start(bf16[768,384]{1,0:T(8,128)(2,1)} %param.13) | copy-start | bytes 1769476
  7.2 35.1 %copy-start.10 = (bf16[96,7,384]{2,0,1:T(8,128)(2,1)S(1)}, bf16[96,7,384]{2,0,1:T(8,128)(2,1)}, u32[]{:S(2)}) copy-start(bf16[96,7,384]{2,0,1:T(8,128)(2,1)} %param.8) | copy-start | bytes 1548292
  8.4 33.8 %copy-start.28 = (f32[1,384,192]{1,2,0:T(8,128)}, f32[1,384,192]{1,2,0:T(8,128)S(1)}, u32[]{:S(2)}) copy-start(f32[1,384,192]{1,2,0:T(8,128)S(1)} %get-tuple-element.86) | copy-start | bytes 884740
  8.4 33.8 %copy-start.30 = (f32[1,384,192]{1,2,0:T(8,128)}, f32[1,384,192]{1,2,0:T(8,128)S(1)}, u32[]{:S(2)}) copy-start(f32[1,384,192]{1,2,0:T(8,128)S(1)} %get-tuple-element.87) | copy-start | bytes 884740
  42.2 136.2 %copy-start.39 = (f32[7,384]{1,0:T(8,128)}, f32[7,384]{1,0:T(8,128)S(1)}, u32[]{:S(2)}) copy-start(f32[7,384]{1,0:T(8,128)S(1)} %get-tuple-element.81) | copy-start | bytes 32260
  107.2 1.8 copy-start.34
  109.0 2.9 copy-start.4
  109.0 2.2 copy-start.35
  112.5 1.6 copy-start.19
  125.9 3.3 copy-start.15
  135.4 41.2 %all-to-all-start.1 = ((f32[96,2,6,224]{0,1,2,3:T(2,128)}), f32[96,2,6,224]{0,1,2,3:T(2,128)}, u32[]{:S(2)}, u32[]{:S(2)}) async-start(f32[96,2,6,224]{0,1,2,3:T(2,128)} %copy.165), calls=%async_computation.1 | async-start | bytes 2752512 | tf_op jit(solution)/shard_map/all_to_all | solution.py:89
  140.1 163.1 %all-gather.3.cloned.1.call-start = ((), (), s32[]{:S(2)}) async-start(), calls=%async_computation.6 | async-start | bytes 4644864 | tf_op jit(solution)/shard_map/all_gather | solution.py:165
  141.3 37.1 %copy-start.24 = (f32[1,192,384]{2,1,0:T(8,128)}, f32[1,192,384]{2,1,0:T(8,128)S(1)}, u32[]{:S(2)}) copy-start(f32[1,192,384]{2,1,0:T(8,128)S(1)} %get-tuple-element.88) | copy-start | bytes 884740
  141.3 37.1 %copy-start.26 = (f32[1,192,384]{2,1,0:T(8,128)}, f32[1,192,384]{2,1,0:T(8,128)S(1)}, u32[]{:S(2)}) copy-start(f32[1,192,384]{2,1,0:T(8,128)S(1)} %get-tuple-element.89) | copy-start | bytes 884740
  176.5 1.9 copy-start.41
  178.4 34.7 %copy-start.42 = (f32[96]{0:T(128)S(1)}, f32[96]{0:T(128)}, u32[]{:S(2)}) copy-start(f32[96]{0:T(128)} %param.12) | copy-start | bytes 1156
  216.3 181.3 %all-gather.5.cloned.1.call-start = ((), (), s32[]{:S(2)}) async-start(), calls=%async_computation.7 | async-start | bytes 4644864 | tf_op jit(solution)/shard_map/all_gather | solution.py:180
  217.6 180.1 %copy-start.45 = (bf16[384,768]{1,0:T(8,128)(2,1)S(1)}, bf16[384,768]{1,0:T(8,128)(2,1)}, u32[]{:S(2)}) copy-start(bf16[384,768]{1,0:T(8,128)(2,1)} %param.14) | copy-start | bytes 1769476
  217.6 374.4 %reduce-scatter.9.cloned.1.call-start = ((), (), s32[]{:S(2)}) async-start(), calls=%async_computation.9 | async-start | bytes 9289728 | tf_op jit(solution)/shard_map/reduce_scatter | solution.py:189
  405.8 1.3 copy-start.22
  422.9 202.1 %copy-start.21 = (bf16[7,12,8,384]{3,2,0,1:T(8,128)(2,1)S(1)}, bf16[7,12,8,384]{3,2,0,1:T(8,128)(2,1)}, u32[]{:S(2)}) copy-start(bf16[7,12,8,384]{3,2,0,1:T(8,128)(2,1)} %copy.214) | copy-start | bytes 1548292
  625.1 2.6 copy-start.29
  625.1 2.6 copy-start.31
  632.4 10.4 copy-start.46
  632.4 46.8 %all-to-all-start.2 = ((f32[96,2,192,7]{0,1,3,2:T(2,128)}), f32[96,2,192,7]{0,1,3,2:T(2,128)}, u32[]{:S(2)}, u32[]{:S(2)}) async-start(f32[96,2,192,7]{0,1,3,2:T(2,128)} %copy.177), calls=%async_computation.2 | async-start | bytes 2752512 | tf_op jit(solution)/shard_map/all_to_all | solution.py:68
  642.7 121.7 %reduce-scatter.7.cloned.1.call-start = ((), (), s32[]{:S(2)}) async-start(), calls=%async_computation.8 | async-start | bytes 4644864 | tf_op jit(solution)/shard_map/reduce_scatter | solution.py:168
  655.2 5.9 copy-start.23
  655.2 5.9 copy-start.44
  682.1 4.1 copy-start.13
  688.8 37.8 %copy-start.6 = (f32[96,1344]{1,0:T(8,128)}, f32[96,1344]{1,0:T(8,128)S(1)}, u32[]{:S(2)}) copy-start(f32[96,1344]{1,0:T(8,128)S(1)} %reshape.642) | copy-start | bytes 1548292
  695.2 3.7 copy-start.8
  695.2 3.0 copy-start.33
  698.3 1.3 copy-start.18
  698.3 1.3 copy-start.20
  709.4 2.8 copy-start.14
  712.2 3.5 copy-start.16
  721.9 44.5 %all-to-all-start.3 = ((f32[96,2,6,224]{0,1,2,3:T(2,128)}), f32[96,2,6,224]{0,1,2,3:T(2,128)}, u32[]{:S(2)}, u32[]{:S(2)}) async-start(f32[96,2,6,224]{0,1,2,3:T(2,128)} %copy.187), calls=%async_computation.3 | async-start | bytes 2752512 | tf_op jit(solution)/shard_map/all_to_all | solution.py:89
  726.6 316.4 %all-reduce.8.cloned.1.call-start = ((), (), s32[]{:S(2)}) async-start(), calls=%async_computation.10 | async-start | bytes 5111808 | tf_op jit(solution)/shard_map/psum | solution.py:213
  727.7 1.3 copy-start.7
  729.1 1.3 copy-start.5
  766.4 2.0 copy-start.3
  766.4 2.0 copy-start.11
  766.4 2.0 copy-start.25
  766.4 2.0 copy-start.27
  766.5 2.0 copy-start.40
  768.5 2.8 copy-start.43
  1043.0 5.6 copy-start.37
  1046.2 3.4 copy-start.1
  (7 other events, 7.2 us)
Sparse Core Ops, SparseCore 0:
  216.5 86.6 all-gather.2
  305.5 92.0 all-gather.4
  421.7 170.2 reduce-scatter.8
  655.3 109.0 reduce-scatter.6
  767.8 275.1 all-reduce.7
where the time goes:
time: 1060 us
  waiting for transfers between devices  589 us (56%)
  blocking collectives  246 us (23%)
  matrix products  107 us (10%)
  local copies, waits for them, and re-layouts  63.4 us (6%)
  starting transfers between devices  19.9 us (2%)
  other arithmetic  16.3 us (2%)
  between operations  14.9 us (1%)
    reduce_scatter x1, waiting for transfers between devices, body(): lax.psum_scatter(jnp.dot(fc_in, grad_pre, preferred_element_type=jnp.floa...  169 us
    psum x1, waiting for transfers between devices, body(): lax.psum((grad_fc_in, grad_fc_out, grad_gain_second, grad_w_inner, grad_w...  168 us
    all_gather x1, waiting for transfers between devices, body(): grad_full = lax.all_gather(grad_rows, 'ch', axis=0, tiled=True)  86.4 us
    all_gather x1, waiting for transfers between devices, body(): inputs_full = lax.all_gather(mlp_input, 'ch', axis=0, tiled=True)  85.6 us
    psum x1, blocking collectives, body(): lax.psum((grad_fc_in, grad_fc_out, grad_gain_second, grad_w_inner, grad_w...  69.8 us
    psum x2, blocking collectives, norm_back(): lax.psum((jnp.sum(gradient, 0), jnp.sum(gradient * normed, 0)), 'ch')  64 us
    psum x2, blocking collectives, normalize(): lax.psum((jnp.sum(values, 0), jnp.sum(values * values, 0)), 'ch')  63.2 us
    all_to_all x1, blocking collectives, to_modes(): lax.all_to_all(spectrum, 'lat', split_axis=2, concat_axis=3, tiled=True)  49.3 us
  transfers between devices with their start and end apart: 8, of which 7 were waited for; matrix products, arithmetic and copies ran while one was open for 8% of the time, Pallas kernels for 0%

commit v1 on v0

v1 whole, which is shorter than its diff:
```python
import math

import jax
import jax.numpy as jnp
import ml_dtypes
import numpy as np
from jax import lax
from jax.experimental import pallas as pl
from jax.experimental.pallas import tpu as pltpu
from jax.sharding import PartitionSpec as P

C = 768
BS = 96
H = 224
W = 384
KW = 192
N_LAT = 32
N_CH = 8
ROWS = 7
FF_DEV = 384
MODES = KW // N_LAT
PLANES = 2 * MODES
LANES = PLANES * BS
GROUP = 384
EPSILON = 1e-05
BF16 = jnp.bfloat16
F32 = jnp.float32
VMEM_BYTES = 56 * 1024 * 1024


def halves(table):
    high = table.astype(ml_dtypes.bfloat16)
    low = (table - high.astype(np.float64)).astype(ml_dtypes.bfloat16)
    return high, low


def lon_table():
    mode = np.arange(MODES)[:, None] + MODES * np.arange(N_LAT)[None, :]
    angles = 2 * np.pi * ((mode[:, :, None] * np.arange(W)) % W) / W
    table = np.stack([np.cos(angles), -np.sin(angles)], 1) / math.sqrt(W)
    return table.reshape(PLANES * N_LAT, W)


def lat_tables():
    index = np.arange(H)
    angles = 2 * np.pi * ((index[:, None] * index[None, :]) % H) / H
    cosine = np.cos(angles) / math.sqrt(H)
    sine = np.sin(angles) / math.sqrt(H)
    forward = np.zeros((H, 2, N_LAT, 8))
    forward[:, 0, :, :ROWS] = cosine.reshape(H, N_LAT, ROWS)
    forward[:, 1, :, :ROWS] = sine.reshape(H, N_LAT, ROWS)
    inverse = np.zeros((N_LAT, 8, 2, H))
    inverse[:, :ROWS, 0] = cosine.reshape(N_LAT, ROWS, H)
    inverse[:, :ROWS, 1] = -sine.reshape(N_LAT, ROWS, H)
    return forward.reshape(H, 2 * N_LAT * 8), inverse.reshape(N_LAT * 8, 2 * H)


def swap_table():
    table = np.zeros((GROUP, GROUP))
    for mode in range(2):
        for c in range(BS):
            real = mode * 2 * BS + c
            table[real + BS, real] = 1
            table[real, real + BS] = -1
    return table.astype(ml_dtypes.bfloat16)


def dot(left, right):
    return lax.dot_general(left, right, (((1,), (0,)), ((), ())), preferred_element_type=F32)


def dot_nt(left, right):
    return lax.dot_general(left, right, (((1,), (1,)), ((), ())), preferred_element_type=F32)


def dot_tn(left, right):
    return lax.dot_general(left, right, (((0,), (0,)), ((), ())), preferred_element_type=F32)


def split(values):
    high = values.astype(BF16)
    return high, (values - high.astype(F32)).astype(BF16)


def dot3(kind, left, right):
    return kind(left[0], right[0]) + kind(left[1], right[0]) + kind(left[0], right[1])


def gelu_parts(values):
    cdf = 0.5 * (1.0 + lax.erf(values * 0.7071067811865476))
    return values * cdf, cdf + values * 0.3989422804014327 * jnp.exp(-0.5 * values * values)


def gelu_value(values):
    return 0.5 * values * (1.0 + lax.erf(values * 0.7071067811865476))


def norm_rows(stats):
    total = stats[0]
    for e in range(1, N_CH):
        total = total + stats[e]
    average = total[0:8] * (1.0 / C)
    squares = total[8:16] * (1.0 / C)
    return average, lax.rsqrt(squares - average * average + EPSILON)


def put_row(scratch, row, modes):
    wide = jnp.concatenate([modes[32 * k : 32 * k + 32] for k in range(PLANES)], axis=1)
    for t in range(LANES // 128):
        scratch[t, pl.ds(row, N_LAT, stride=8), :] = wide[:, 128 * t : 128 * t + 128]


def flush_rows(scratch, wire):
    for t in range(LANES // 128):
        scratch[t, pl.ds(ROWS, N_LAT, stride=8), :] = jnp.zeros((N_LAT, 128), F32)
        wire[:, 128 * t : 128 * t + 128] = scratch[t].astype(BF16)


def load_rows(wire, scratch):
    for t in range(LANES // 128):
        scratch[t] = wire[:, 128 * t : 128 * t + 128].astype(F32)


def get_row(scratch, row):
    wide = jnp.concatenate(
        [scratch[t, pl.ds(row, N_LAT, stride=8), :] for t in range(LANES // 128)], axis=1
    )
    return jnp.concatenate([wide[:, BS * k : BS * k + BS] for k in range(PLANES)], axis=0)


def to_chunk(rows, e):
    return jnp.concatenate(
        [
            jnp.concatenate(
                [values[48 * e + 8 * a : 48 * e + 8 * a + 8] for a in range(6)], axis=1
            )
            for values in rows
        ],
        axis=0,
    )


def from_chunks(chunks, row):
    return jnp.concatenate(
        [
            chunk[8 * row : 8 * row + 8, BS * a : BS * a + BS]
            for chunk in chunks
            for a in range(6)
        ],
        axis=0,
    )


def cot_kernel(cot, wire):
    rows = [cot[r].astype(F32).T for r in range(ROWS)]
    for e in range(N_CH):
        wire[e] = to_chunk(rows, e).astype(BF16)


def lon_kernel(x, stats, gain, t_high, t_low, wire, scratch):
    average, inv_std = norm_rows(stats)
    table = (t_high[...], t_low[...])
    for r in range(ROWS):
        normed = (x[r].astype(F32) - average[r : r + 1]) * inv_std[r : r + 1]
        lifted = split(normed * gain[...])
        put_row(scratch, r, dot3(dot_nt, table, lifted))
    flush_rows(scratch, wire)


def lat_forward(wire, lf_high, lf_low, swap):
    values = wire[...]
    swapped = dot(values, swap[...]).astype(BF16)
    both = jnp.concatenate([values, swapped], axis=0)
    return dot(lf_high[...], both) + dot(lf_low[...], both)


def lat_inverse(modes, li_high, li_low):
    both = split(jnp.concatenate([modes[:, :GROUP], modes[:, GROUP:]], axis=0))
    return dot3(dot, (li_high[...], li_low[...]), both)


def spectral_kernel(
    wire, lf_high, lf_low, swap, m1_high, m1_low, m2_high, m2_low, doubled, li_high, li_low,
    out, spectrum, pre_modes,
):
    modes = lat_forward(wire, lf_high, lf_low, swap)
    spectrum[...] = modes
    pre = dot3(dot, split(modes), (m1_high[...], m1_low[...]))
    pre_modes[...] = pre
    act = split(gelu_value(pre))
    scale = doubled[...]
    result = dot3(dot, act, (m2_high[...], m2_low[...])) * jnp.concatenate([scale, scale], axis=1)
    out[...] = lat_inverse(result, li_high, li_low).astype(BF16)


def spectral_back_kernel(
    wire, spectrum, pre_modes, lf_high, lf_low, swap, m1_high, m1_low, m2_high, m2_low, doubled,
    li_high, li_low, out, grad_outer, grad_inner, gain_part,
):
    @pl.when(pl.program_id(0) == 0)
    def _():
        grad_outer[...] = jnp.zeros_like(grad_outer)
        grad_inner[...] = jnp.zeros_like(grad_inner)

    grad = split(lat_forward(wire, lf_high, lf_low, swap) * doubled[...])
    act, slope = gelu_parts(pre_modes[...])
    grad_act = dot3(dot_nt, grad, (m2_high[:, :GROUP], m2_low[:, :GROUP]))
    grad_outer[...] += dot3(dot_tn, grad, split(act))
    grad_pre = split(grad_act * slope)
    modes = spectrum[...]
    grad_inner[...] += dot3(dot_tn, grad_pre, split(modes))
    grad_spectrum = dot3(dot_nt, grad_pre, (m1_high[...], m1_low[...]))
    gain_part[...] = jnp.sum(grad_spectrum[:, :GROUP] * modes, axis=0, keepdims=True)
    out[...] = lat_inverse(grad_spectrum, li_high, li_low).astype(BF16)


def mix_kernel(wire, tt_high, tt_low, x, stats, gain, mixed, chunks, scratch):
    average, inv_std = norm_rows(stats)
    load_rows(wire, scratch)
    rows = []
    for r in range(ROWS):
        x_float = x[r].astype(F32)
        lifted = (x_float - average[r : r + 1]) * inv_std[r : r + 1] * gain[...]
        modes = get_row(scratch, r).astype(BF16)
        filtered = dot(tt_high[...], modes) + dot(tt_low[...], modes)
        values = filtered + (lifted + x_float).T
        mixed[r] = values
        rows.append(values)
    for e in range(N_CH):
        chunks[e] = to_chunk(rows, e)


def mlp_kernel(
    core, mixed, cot, gain, own, other, out_chunks, grad_chunks, grad_own, grad_other,
    normed, inputs, cots, inv_std, sum_out, sum_grad,
):
    step = pl.program_id(0)
    turn = 4 * core[0]
    cells = 6 * 8 * ROWS
    part = 8 * ROWS

    def gain_row():
        return jnp.concatenate([gain[e ^ turn] for e in range(N_CH)], axis=1)

    @pl.when(step == 0)
    def _():
        pieces = [mixed[e ^ turn] for e in range(N_CH)]
        values = jnp.concatenate(
            [
                jnp.concatenate([piece[:, BS * a : BS * a + BS] for piece in pieces], axis=1)
                for a in range(6)
            ],
            axis=0,
        )
        average = jnp.sum(values, axis=1, keepdims=True) * (1.0 / C)
        squares = jnp.sum(values * values, axis=1, keepdims=True) * (1.0 / C)
        inv = lax.rsqrt(squares - average * average + EPSILON)
        values = (values - average) * inv
        normed[...] = values
        inv_std[...] = jnp.broadcast_to(inv, (cells, 128))
        inputs[...] = (values * gain_row()).astype(BF16)
        pieces = [cot[e ^ turn].astype(F32) for e in range(N_CH)]
        cots[...] = jnp.concatenate(
            [
                jnp.concatenate([piece[:, BS * a : BS * a + BS] for piece in pieces], axis=1)
                for a in range(6)
            ],
            axis=0,
        ).astype(BF16)
        sum_out[...] = jnp.zeros_like(sum_out)
        sum_grad[...] = jnp.zeros_like(sum_grad)

    first, second = inputs[:, :384], inputs[:, 384:]
    cot_first, cot_second = cots[:, :384], cots[:, 384:]
    in_own, out_own = own[0, 0], own[0, 1]
    in_other, out_other = other[0, 0], other[0, 1]
    pre_act = dot(first, in_own) + dot(second, in_other)
    hidden, slope = gelu_parts(pre_act)
    hidden = hidden.astype(BF16)
    grad_hidden = dot_nt(cot_first, out_own) + dot_nt(cot_second, out_other)
    grad_pre = (grad_hidden * slope).astype(BF16)
    sum_out[:, :384] += dot(hidden, out_own)
    sum_out[:, 384:] += dot(hidden, out_other)
    sum_grad[:, :384] += dot_nt(grad_pre, in_own)
    sum_grad[:, 384:] += dot_nt(grad_pre, in_other)
    grad_own[0, 0] = dot_tn(first, grad_pre)
    grad_other[0, 0] = dot_tn(second, grad_pre).astype(BF16)
    grad_own[0, 1] = dot_tn(hidden, cot_first)
    grad_other[0, 1] = dot_tn(hidden, cot_second).astype(BF16)

    @pl.when(step == N_CH - 1)
    def _():
        grad_input = sum_grad[...]
        values = normed[...]
        gain_sum = jnp.sum(grad_input * values, axis=0, keepdims=True)
        scaled = grad_input * gain_row()
        leading = jnp.sum(scaled, axis=1, keepdims=True) * (1.0 / C)
        paired = jnp.sum(scaled * values, axis=1, keepdims=True) * (1.0 / C)
        grad_mixed = cots[...].astype(F32) + inv_std[:, :1] * (scaled - leading - values * paired)
        outputs = sum_out[...]

        def chunk(array, e):
            return jnp.concatenate(
                [array[part * a : part * a + part, BS * e : BS * e + BS] for a in range(6)],
                axis=1,
            )

        for e in range(N_CH):
            out_chunks[e ^ turn] = chunk(outputs, e).astype(BF16)
            gain_piece = gain_sum[:, BS * e : BS * e + BS]
            gain_high = gain_piece.astype(BF16).astype(F32)
            extra = jnp.concatenate(
                [gain_high, gain_piece - gain_high, jnp.zeros((1, 4 * BS), F32)], axis=1
            )
            extra = jnp.concatenate([extra, jnp.zeros((7, 6 * BS), F32)], axis=0)
            grad_chunks[e ^ turn] = jnp.concatenate(
                [chunk(grad_mixed, e), extra], axis=0
            ).astype(BF16)


def lon_back_kernel(chunks, x, stats, t_high, t_low, wire, grad_mixed, gains, scratch):
    average, inv_std = norm_rows(stats)
    pieces = [chunks[e].astype(F32) for e in range(N_CH)]
    gain_first = jnp.zeros((BS, 1), F32)
    for r in range(ROWS):
        values = from_chunks(pieces, r)
        rounded = values.astype(BF16)
        put_row(scratch, r, dot(t_high[...], rounded) + dot(t_low[...], rounded))
        turned = values.T
        grad_mixed[r] = turned.astype(BF16)
        normed = (x[r].astype(F32) - average[r : r + 1]) * inv_std[r : r + 1]
        gain_first = gain_first + jnp.sum(turned * normed, axis=1, keepdims=True)
    flush_rows(scratch, wire)
    gain_second = jnp.zeros((1, BS), F32)
    for piece in pieces:
        row = piece[8 * ROWS : 8 * ROWS + 1]
        gain_second = gain_second + row[:, :BS] + row[:, BS : 2 * BS]
    turned_first = jnp.broadcast_to(gain_first, (BS, 128)).T[0:1, :]
    gains[0:1, :BS] = turned_first
    gains[1:2, :BS] = gain_second


def unmix_kernel(wire, tt_high, tt_low, grad_mixed, x, stats, gain, scaled, sums, scratch):
    average, inv_std = norm_rows(stats)
    load_rows(wire, scratch)
    for r in range(ROWS):
        modes = get_row(scratch, r).astype(BF16)
        back = dot(tt_high[...], modes) + dot(tt_low[...], modes)
        values = (back.T + grad_mixed[r].astype(F32)) * gain[...]
        normed = (x[r].astype(F32) - average[r : r + 1]) * inv_std[r : r + 1]
        scaled[r] = values
        sums[r : r + 1] = jnp.sum(values, axis=0, keepdims=True)
        sums[8 + r : 9 + r] = jnp.sum(values * normed, axis=0, keepdims=True)
    sums[7:8] = jnp.zeros((1, W), F32)
    sums[15:16] = jnp.zeros((1, W), F32)


def final_kernel(scaled, grad_mixed, x, stats, back_stats, out):
    average, inv_std = norm_rows(stats)
    total = back_stats[0]
    for e in range(1, N_CH):
        total = total + back_stats[e]
    total = total * (1.0 / C)
    for r in range(ROWS):
        inv = inv_std[r : r + 1]
        normed = (x[r].astype(F32) - average[r : r + 1]) * inv
        change = scaled[r] - total[r : r + 1] - normed * total[8 + r : 9 + r]
        out[r] = (grad_mixed[r].astype(F32) + inv * change).astype(BF16)


def output_kernel(chunks, mixed, out):
    pieces = [chunks[e].astype(F32) for e in range(N_CH)]
    for r in range(ROWS):
        out[r] = (from_chunks(pieces, r) + mixed[r]).T.astype(BF16)


def call(kernel, out_shape, *args, scratch=(), name=None):
    return pl.pallas_call(
        kernel,
        out_shape=out_shape,
        scratch_shapes=scratch,
        compiler_params=pltpu.CompilerParams(vmem_limit_bytes=VMEM_BYTES),
        name=name,
    )(*args)


def shaped(*shape, dtype=F32):
    return jax.ShapeDtypeStruct(shape, dtype)


def whole(shape):
    return pl.BlockSpec(shape, lambda g: (0,) * len(shape))


def lane_block(rows):
    return pl.BlockSpec((rows, GROUP), lambda g: (0, g))


def block_matrix(weight, swap_columns, swap_rows):
    real, imag = weight[0, 0].T, weight[1, 0].T
    base = [[real, imag], [-imag, real]]
    if swap_columns:
        base = [[imag, -real], [real, imag]]
    if swap_rows:
        base = [[-imag, real], [-real, -imag]]
    one = jnp.concatenate([jnp.concatenate(line, axis=1) for line in base], axis=0)
    zero = jnp.zeros_like(one)
    return jnp.concatenate(
        [jnp.concatenate([one, zero], axis=1), jnp.concatenate([zero, one], axis=1)], axis=0
    )


def weight_sum(blocks):
    parts = blocks.reshape(2, 2, BS, 2, 2, BS)
    parts = parts[0, :, :, 0] + parts[1, :, :, 1]
    return jnp.stack(
        [parts[0, :, 0] + parts[1, :, 1], parts[1, :, 0] - parts[0, :, 1]], axis=0
    )


def to_all(values, axis, count, **kwargs):
    spread = jnp.broadcast_to(values[None], (count,) + values.shape)
    return lax.all_to_all(spread, axis, 0, 0, tiled=True, **kwargs)


def body(fields, gain_first, w_inner, w_outer, gain_second, fc_in, fc_out, cotangent):
    lat = lax.axis_index("lat")
    core = lat % 2
    siblings = [(i, i ^ 1) for i in range(N_LAT)]
    cores = [list(range(0, N_LAT, 2)), list(range(1, N_LAT, 2))]
    t_high, t_low = (jnp.asarray(t) for t in halves(lon_table()))
    tt_high, tt_low = (jnp.asarray(t) for t in halves(lon_table().T))
    forward, inverse = lat_tables()
    lf_high, lf_low = (jnp.asarray(t) for t in halves(forward))
    li_high, li_low = (jnp.asarray(t) for t in halves(inverse))
    swap = jnp.asarray(swap_table())

    x = fields.transpose(1, 0, 2)
    cot = cotangent.transpose(1, 0, 2)
    gain_column = gain_first[:, None]

    with jax.named_scope("weights"):
        half_in = lax.dynamic_slice_in_dim(fc_in, core * 384, 384, 0)
        half_out = lax.dynamic_slice_in_dim(fc_out, core * 384, 384, 1)
        own = lax.all_gather(jnp.stack([half_in, half_out]), "ch")
        other = lax.ppermute(own, "lat", siblings)

    with jax.named_scope("stats"):
        x_float = x.astype(F32)
        zero = jnp.zeros((1, W), F32)
        payload = jnp.concatenate(
            [
                jnp.sum(x_float, 1),
                zero,
                jnp.sum(x_float * x_float, 1),
                zero,
                jnp.pad(gain_second, (0, W - BS))[None],
                jnp.zeros((7, W), F32),
            ],
            axis=0,
        )
        gathered = to_all(payload, "ch", N_CH)
        stats = gathered[:, :16]
        gains = gathered[:, 16:17, :BS]

    scratch = pltpu.VMEM((LANES // 128, 8 * N_LAT, 128), F32)
    wire_shape = shaped(8 * N_LAT, LANES, dtype=BF16)
    with jax.named_scope("lon"):
        wire = call(
            lon_kernel, wire_shape, x, stats, gain_column, t_high, t_low, scratch=[scratch]
        )
        wire = lax.all_to_all(wire, "lat", 0, 0, tiled=True)

    with jax.named_scope("cot"):
        cot_chunks = call(cot_kernel, shaped(N_CH, 8 * ROWS, 6 * BS, dtype=BF16), cot)
        cot_chunks = lax.all_to_all(cot_chunks, "ch", 0, 0, tiled=True)

    with jax.named_scope("matrices"):
        m1 = split(
            jnp.concatenate(
                [block_matrix(w_inner, False, False), block_matrix(w_inner, False, True)], axis=0
            )
        )
        m2 = split(
            jnp.concatenate(
                [block_matrix(w_outer, False, False), block_matrix(w_outer, True, False)], axis=1
            )
        )
        lane = jnp.arange(LANES, dtype=jnp.int32)[None]
        doubled = jnp.where((lat == 0) & (lane < 2 * BS), 1.0, 2.0).astype(F32)

    table_specs = [whole((H, 512)), whole((H, 512)), whole((GROUP, GROUP))]
    inverse_specs = [lane_block(1), whole((256, 448)), whole((256, 448))]
    params = pltpu.CompilerParams(vmem_limit_bytes=VMEM_BYTES)
    with jax.named_scope("spectral"):
        wire, spectrum, pre_modes = pl.pallas_call(
            spectral_kernel,
            grid=(3,),
            in_specs=[lane_block(256)]
            + table_specs
            + [whole((GROUP, GROUP))] * 2
            + [whole((GROUP, 2 * GROUP))] * 2
            + inverse_specs,
            out_specs=[lane_block(256), lane_block(H), lane_block(H)],
            out_shape=[wire_shape, shaped(H, LANES), shaped(H, LANES)],
            compiler_params=params,
        )(
            wire, lf_high, lf_low, swap, m1[0][:GROUP], m1[1][:GROUP], m2[0], m2[1], doubled,
            li_high, li_low,
        )
        wire = lax.all_to_all(wire, "lat", 0, 0, tiled=True)

    with jax.named_scope("mix"):
        mixed, chunks = call(
            mix_kernel,
            [shaped(ROWS, W, BS), shaped(N_CH, 8 * ROWS, 6 * BS)],
            wire, tt_high, tt_low, x, stats, gain_column,
            scratch=[scratch],
        )
        chunks = lax.all_to_all(chunks, "ch", 0, 0, tiled=True)

    cells = 48 * ROWS
    weight_spec = pl.BlockSpec((1, 2, 384, 384), lambda e: (e, 0, 0, 0))
    with jax.named_scope("mlp"):
        out_chunks, grad_chunks, grad_own, grad_other = pl.pallas_call(
            mlp_kernel,
            grid=(N_CH,),
            in_specs=[
                pl.BlockSpec(memory_space=pltpu.SMEM),
                whole((N_CH, 8 * ROWS, 6 * BS)),
                whole((N_CH, 8 * ROWS, 6 * BS)),
                whole((N_CH, 1, BS)),
                weight_spec,
                weight_spec,
            ],
            out_specs=[
                whole((N_CH, 8 * ROWS, 6 * BS)),
                whole((N_CH, 8 * ROWS + 8, 6 * BS)),
                weight_spec,
                weight_spec,
            ],
            out_shape=[
                shaped(N_CH, 8 * ROWS, 6 * BS, dtype=BF16),
                shaped(N_CH, 8 * ROWS + 8, 6 * BS, dtype=BF16),
                shaped(N_CH, 2, 384, 384),
                shaped(N_CH, 2, 384, 384, dtype=BF16),
            ],
            scratch_shapes=[
                pltpu.VMEM((cells, C), F32),
                pltpu.VMEM((cells, C), BF16),
                pltpu.VMEM((cells, C), BF16),
                pltpu.VMEM((cells, 128), F32),
                pltpu.VMEM((cells, C), F32),
                pltpu.VMEM((cells, C), F32),
            ],
            compiler_params=params,
        )(core[None].astype(jnp.int32), chunks, cot_chunks, gains, own, other)
        grad_chunks = lax.all_to_all(grad_chunks, "ch", 0, 0, tiled=True)

    with jax.named_scope("lon_back"):
        wire, grad_mixed, gain_parts = call(
            lon_back_kernel,
            [wire_shape, shaped(ROWS, BS, W, dtype=BF16), shaped(8, 128)],
            grad_chunks, x, stats, t_high, t_low,
            scratch=[scratch],
        )
        wire = lax.all_to_all(wire, "lat", 0, 0, tiled=True)

    with jax.named_scope("output"):
        out_chunks = lax.all_to_all(out_chunks, "ch", 0, 0, tiled=True)
        output = call(output_kernel, shaped(ROWS, BS, W, dtype=BF16), out_chunks, mixed)

    with jax.named_scope("spectral_back"):
        wire, blocks_outer, blocks_inner, gain_modes = pl.pallas_call(
            spectral_back_kernel,
            grid=(3,),
            in_specs=[lane_block(256), lane_block(H), lane_block(H)]
            + table_specs
            + [whole((2 * GROUP, GROUP))] * 2
            + [whole((GROUP, 2 * GROUP))] * 2
            + inverse_specs,
            out_specs=[lane_block(256), whole((GROUP, GROUP)), whole((GROUP, GROUP)), lane_block(1)],
            out_shape=[wire_shape, shaped(GROUP, GROUP), shaped(GROUP, GROUP), shaped(1, LANES)],
            compiler_params=params,
        )(
            wire, spectrum, pre_modes, lf_high, lf_low, swap, m1[0], m1[1], m2[0], m2[1], doubled,
            li_high, li_low,
        )
        wire = lax.all_to_all(wire, "lat", 0, 0, tiled=True)

    with jax.named_scope("unmix"):
        scaled, sums = call(
            unmix_kernel,
            [shaped(ROWS, BS, W), shaped(16, W)],
            wire, tt_high, tt_low, grad_mixed, x, stats, gain_column,
            scratch=[scratch],
        )
        back_stats = to_all(sums, "ch", N_CH)
        grad_fields = call(
            final_kernel, shaped(ROWS, BS, W, dtype=BF16), scaled, grad_mixed, x, stats, back_stats
        )

    with jax.named_scope("small_grads"):
        grad_gain_first = gain_parts[0, :BS] + (
            jnp.sum(gain_modes.reshape(PLANES, BS), 0) / gain_first
        )
        flat = jnp.concatenate(
            [
                weight_sum(blocks_inner).reshape(-1),
                weight_sum(blocks_outer).reshape(-1),
                grad_gain_first,
                gain_parts[1, :BS],
            ]
        )
        count = flat.shape[0]
        padded = -(-count // (N_LAT * 128)) * N_LAT * 128
        flat = jnp.pad(flat, (0, padded - count)).reshape(N_LAT, padded // N_LAT // 128, 128)
        flat = jnp.sum(lax.all_to_all(flat, "lat", 0, 0, tiled=True), 0)
        flat = to_all(flat, "lat", N_LAT).reshape(-1)
        size = 2 * BS * BS
        grad_w_inner = flat[:size].reshape(2, 1, BS, BS)
        grad_w_outer = flat[size : 2 * size].reshape(2, 1, BS, BS)
        grad_gain_first = flat[2 * size : 2 * size + BS]
        grad_gain_second = flat[2 * size + BS : 2 * size + 2 * BS]

    with jax.named_scope("weight_grads"):
        received = lax.ppermute(grad_other, "lat", siblings)
        partial = (grad_own + received.astype(F32)).astype(BF16)
        partial = lax.all_to_all(partial, "ch", 0, 0, tiled=True)
        partial = jnp.sum(partial.astype(F32), 0).astype(BF16).reshape(N_LAT // 2, 48, 384)
        partial = lax.all_to_all(partial, "lat", 0, 0, tiled=True, axis_index_groups=cores)
        partial = jnp.sum(partial.astype(F32), 0).astype(BF16)
        mine = to_all(partial, "lat", N_LAT // 2, axis_index_groups=cores)
        mine = mine.reshape(2, 384, 384)
        theirs = lax.ppermute(mine, "lat", siblings)
        low = jnp.where(core == 0, mine, theirs).astype(F32)
        high = jnp.where(core == 0, theirs, mine).astype(F32)
        grad_fc_in = jnp.concatenate([low[0], high[0]], axis=0)
        grad_fc_out = jnp.concatenate([low[1], high[1]], axis=1)

    return (
        output.transpose(1, 0, 2),
        grad_fields.transpose(1, 0, 2),
        grad_gain_first,
        grad_w_inner,
        grad_w_outer,
        grad_gain_second,
        grad_fc_in,
        grad_fc_out,
    )


def solution(mesh):
    placed = (
        P("ch", "lat", None),
        P("ch"),
        P(None, "ch", None, None),
        P(None, "ch", None, None),
        P("ch"),
        P(None, "ch"),
        P("ch", None),
        P("ch", "lat", None),
    )
    return jax.shard_map(
        body,
        mesh=mesh,
        in_specs=placed,
        out_specs=(
            P("ch", "lat", None),
            P("ch", "lat", None),
            P("ch"),
            P(None, "ch", None, None),
            P(None, "ch", None, None),
            P("ch"),
            P(None, "ch"),
            P("ch", None),
        ),
        check_vma=False,
    )
```

time: 1060 us -> 517 us (0.49)
  waiting for transfers between devices: 589 us -> 277 us
  blocking collectives: 246 us -> 40 us
  matrix products: 107 us -> 0 us
  Pallas kernels: 0 us -> 72.6 us
  starting transfers between devices: 19.9 us -> 70.7 us
  local copies, waits for them, and re-layouts: 63.4 us -> 19 us
    reduce_scatter x2 -> x0, waiting for transfers between devices: 199 us -> none  [the longest x1 169 us: body(): lax.psum_scatter(jnp.dot(fc_in, grad_pre, preferred_element_type=jnp.floa...]
    psum x5 -> x0, blocking collectives: 197 us -> none  [the longest x1 69.8 us: body(): lax.psum((grad_fc_in, grad_fc_out, grad_gain_second, grad_w_inner, grad_w...]
    psum x1 -> x0, waiting for transfers between devices: 168 us -> none  [body(): lax.psum((grad_fc_in, grad_fc_out, grad_gain_second, grad_w_inner, grad_w...]
    all_to_all x3 -> x13, waiting for transfers between devices: 50 us -> 171 us  [the longest x4 65.3 us: body(): wire = lax.all_to_all(wire, 'lat', 0, 0, tiled=True)]
    dot_general x50 -> x0, matrix products: 107 us -> none  [the longest x16 34.2 us: matmul_high(): return jnp.matmul(left, right, precision=HIGHEST)]
    pallas_call x0 -> x10, Pallas kernels: none -> 72.6 us  [the longest x1 24.7 us: body(): pl.pallas_call(mlp_kernel, grid=(N_CH,), in_specs=[pl.BlockSpec(memory_sp...]
    all_gather x2 -> x1, waiting for transfers between devices: 172 us -> 106 us  [body(): own = lax.all_gather(jnp.stack([half_in, half_out]), 'ch')]
    all_to_all x3 -> x13, starting transfers between devices: 19.7 us -> 70.4 us  [the longest x4 24.2 us: body(): wire = lax.all_to_all(wire, 'lat', 0, 0, tiled=True)]
  transfers between devices with their start and end apart: 8 -> 17, of which waited for: 7 -> 14; matrix products, arithmetic and copies ran while one was open for 8% -> 6% of each run, Pallas kernels for 0% -> 9%
where the time goes in v1:
time: 517 us; the launch traced here: 514 us
  waiting for transfers between devices  277 us (54%)
  Pallas kernels  72.6 us (14%)
  starting transfers between devices  70.7 us (14%)
  blocking collectives  40 us (8%)
  other arithmetic  20.3 us (4%)
  local copies, waits for them, and re-layouts  19 us (4%)
  between operations  14.5 us (3%)
    all_gather x1, waiting for transfers between devices, body(): own = lax.all_gather(jnp.stack([half_in, half_out]), 'ch')  106 us
    all_to_all x4, waiting for transfers between devices, body(): wire = lax.all_to_all(wire, 'lat', 0, 0, tiled=True)  65.3 us
    all_to_all x1, waiting for transfers between devices, body(): partial = lax.all_to_all(partial, 'ch', 0, 0, tiled=True)  32.7 us
    pallas_call x1, Pallas kernels, body(): pl.pallas_call(mlp_kernel, grid=(N_CH,), in_specs=[pl.BlockSpec(memory_sp...  24.7 us
    all_to_all x3, waiting for transfers between devices, to_all(): return lax.all_to_all(spread, axis, 0, 0, tiled=True, **kwargs)  24.3 us
    pallas_call x7, Pallas kernels, call(): pl.pallas_call(kernel, out_shape=out_shape, scratch_shapes=scratch, compi...  24.3 us
    all_to_all x4, starting transfers between devices, body(): wire = lax.all_to_all(wire, 'lat', 0, 0, tiled=True)  24.2 us
    all_to_all x1, blocking collectives, to_all(): return lax.all_to_all(spread, axis, 0, 0, tiled=True, **kwargs)  22.8 us
  transfers between devices with their start and end apart: 17, of which 14 were waited for; matrix products, arithmetic and copies ran while one was open for 6% of the time, Pallas kernels for 9%

profile of v1, /device:TPU:8, one launch (start us, length us, event | category | flops | bytes accessed | tf_op | source)
XLA Modules:
  0.0 514.1 jit_solution(12567862450712685825)
XLA Ops:
  7.2 1.1 dynamic-slice_bitcast_fusion
  9.3 106.1 %all-gather.3.cloned.1.call-done = bf16[16,384,384]{2,1,0:T(8,128)(2,1)} async-done(((bf16[2,384,384]{2,1,0:T(8,128)(2,1)}), bf16[16,384,384]{2,1,0:T(8,128)(2,1)}) %all-gather.3.cloned.1.call-update) | async-done | bytes 4718608 | tf_op jit(solution)/shard_map/weights/all_gather | solution.py:445
  116.4 5.4 %all-to-all-start = ((f32[8,24,384]{2,1,0:T(8,128)}), f32[8,24,384]{2,1,0:T(8,128)S(1)}, u32[]{:S(2)}, u32[]{:S(2)}) async-start(f32[8,24,384]{2,1,0:T(8,128)} %broadcast_in_dim.52), calls=%async_computation | async-start | bytes 589824 | tf_op jit(solution)/shard_map/stats/all_to_all | solution.py:423
  123.2 5.0 all-to-all-done
  128.9 4.2 lon.1
  133.1 9.8 %all-to-all-start.1 = ((bf16[32,8,1152]{2,1,0:T(8,128)(2,1)}), bf16[32,8,1152]{2,1,0:T(8,128)(2,1)S(1)}, u32[]{:S(2)}, u32[]{:S(2)}) async-start(bf16[32,8,1152]{2,1,0:T(8,128)(2,1)} %bitcast.78), calls=%async_computation.1 | async-start | bytes 1179648 | tf_op jit(solution)/shard_map/lon/all_to_all | solution.py:472
  145.5 1.3 subtract_convert_fusion
  146.8 17.2 %all-to-all-done.1 = bf16[32,8,1152]{2,1,0:T(8,128)(2,1)S(1)} async-done(((bf16[32,8,1152]{2,1,0:T(8,128)(2,1)}), bf16[32,8,1152]{2,1,0:T(8,128)(2,1)S(1)}, u32[]{:S(2)}, u32[]{:S(2)}) %all-to-all-start.1) | async-done | bytes 589856 | tf_op jit(solution)/shard_map/lon/all_to_all | solution.py:472
  164.8 10.7 %spectral.1 = (bf16[256,1152]{1,0:T(8,128)(2,1)}, f32[224,1152]{1,0:T(8,128)}, f32[224,1152]{1,0:T(8,128)}) custom-call(bf16[256,1152]{1,0:T(8,128)(2,1)} %bitcast.75, bf16[224,512]{1,0:T(8,128)(2,1)} %constant.61.clone.lf_high, bf16[224,512]{1,0:T(8,128)(2,1)} %constant.62.clone.lf_low, bf16[384,384]{1,0:T(8,128)(2,1)} %constant.65.clone.swap, ...), custom_call_target="tpu_custom_call" | custom-call | tf_op jit(solution)/shard_map/spectral/pallas_call | solution.py:496
  175.4 3.9 all-to-all-start.2
  179.3 2.3 cot.1
  181.6 18.9 %all-to-all-done.2 = bf16[32,8,1152]{2,1,0:T(8,128)(2,1)S(1)} async-done(((bf16[32,8,1152]{2,1,0:T(8,128)(2,1)}), bf16[32,8,1152]{2,1,0:T(8,128)(2,1)S(1)}, u32[]{:S(2)}, u32[]{:S(2)}) %all-to-all-start.2) | async-done | bytes 589856 | tf_op jit(solution)/shard_map/spectral/all_to_all | solution.py:511
  200.5 5.4 %all-to-all-start.4 = ((bf16[8,56,576]{2,1,0:T(8,128)(2,1)}), bf16[8,56,576]{2,1,0:T(8,128)(2,1)S(1)}, u32[]{:S(2)}, u32[]{:S(2)}) async-start(bf16[8,56,576]{2,1,0:T(8,128)(2,1)} %cot.1), calls=%async_computation.4 | async-start | bytes 1146880 | tf_op jit(solution)/shard_map/cot/all_to_all | solution.py:476
  205.9 4.3 mix.1
  210.2 3.2 all-to-all-done.4.cot
  213.4 5.4 %all-to-all-start.3 = ((f32[8,56,576]{2,1,0:T(8,128)}), f32[8,56,576]{2,1,0:T(8,128)S(1)}, u32[]{:S(2)}, u32[]{:S(2)}) async-start(f32[8,56,576]{2,1,0:T(8,128)} %get-tuple-element.27), calls=%async_computation.3 | async-start | bytes 2293760 | tf_op jit(solution)/shard_map/mix/all_to_all | solution.py:520
  219.4 12.0 %all-to-all-done.3.mixed = f32[8,56,576]{2,1,0:T(8,128)S(1)} async-done(((f32[8,56,576]{2,1,0:T(8,128)}), f32[8,56,576]{2,1,0:T(8,128)S(1)}, u32[]{:S(2)}, u32[]{:S(2)}) %all-to-all-start.3) | async-done | bytes 1032224 | tf_op jit(solution)/shard_map/mix/all_to_all | solution.py:520
  231.5 1.0 copy-done.1
  232.5 24.7 %mlp.1 = (bf16[8,56,576]{2,1,0:T(8,128)(2,1)}, bf16[8,64,576]{2,1,0:T(8,128)(2,1)}, f32[8,2,384,384]{3,2,1,0:T(8,128)}, bf16[8,2,384,384]{3,2,1,0:T(8,128)(2,1)}) custom-call(s32[1]{0:T(128)} %bitcast.core, f32[8,56,576]{2,1,0:T(8,128)} %copy-done.1, bf16[8,56,576]{2,1,0:T(8,128)(2,1)} %copy-done.9, f32[8,1,96]{2,1,0:T(1,128)} %slice.127.gain, ...), custom_call_target="tpu_custom_call" | custom-call | tf_op jit(solution)/shard_map/mlp/pallas_call | solution.py:525
  257.1 17.2 %all_to_all.99.chunks = bf16[8,64,576]{2,1,0:T(8,128)(2,1)} all-to-all(bf16[8,64,576]{2,1,0:T(8,128)(2,1)} %get-tuple-element.30), channel_id=1, replica_groups=mesh['lat'=32,'ch'=8] {'ch'}, dimensions={0} | all-to-all | bytes 1179648 | tf_op jit(solution)/shard_map/mlp/all_to_all | solution.py:558
  274.4 5.0 all-to-all-start.5
  279.4 3.8 lon_back.1
  283.3 4.8 all-to-all-done.5.chunks
  288.1 6.6 %all-to-all-start.7 = ((bf16[32,8,1152]{2,1,0:T(8,128)(2,1)}), bf16[32,8,1152]{2,1,0:T(8,128)(2,1)S(1)}, u32[]{:S(2)}, u32[]{:S(2)}) async-start(bf16[32,8,1152]{2,1,0:T(8,128)(2,1)} %bitcast.82), calls=%async_computation.7 | async-start | bytes 1179648 | tf_op jit(solution)/shard_map/lon_back/all_to_all | solution.py:567
  294.7 8.4 %add_convert_fusion = bf16[8,2,384,384]{3,2,1,0:T(8,128)(2,1)} fusion(f32[8,2,384,384]{3,2,1,0:T(8,128)} %get-tuple-element.42, bf16[8,2,384,384]{3,2,1,0:T(8,128)(2,1)} %collective-permute-done.1), kind=kLoop, calls=%fused_computation | loop fusion | flops 7077888 | bytes 18874368 | tf_op jit(solution)/shard_map/weight_grads/convert_element_type | solution.py:628
  303.1 12.6 %all-to-all-done.7 = bf16[32,8,1152]{2,1,0:T(8,128)(2,1)S(1)} async-done(((bf16[32,8,1152]{2,1,0:T(8,128)(2,1)}), bf16[32,8,1152]{2,1,0:T(8,128)(2,1)S(1)}, u32[]{:S(2)}, u32[]{:S(2)}) %all-to-all-start.7) | async-done | bytes 589856 | tf_op jit(solution)/shard_map/lon_back/all_to_all | solution.py:567
  316.6 6.6 %all-to-all-start.12 = ((bf16[8,2,384,384]{3,2,1,0:T(8,128)(2,1)}), bf16[8,2,384,384]{3,2,1,0:T(8,128)(2,1)}, u32[]{:S(2)}, u32[]{:S(2)}) async-start(bf16[8,2,384,384]{3,2,1,0:T(8,128)(2,1)} %add_convert_fusion), calls=%async_computation.12 | async-start | bytes 9437184 | tf_op jit(solution)/shard_map/weight_grads/all_to_all | solution.py:629
  323.8 13.0 %spectral_back.1 = (bf16[256,1152]{1,0:T(8,128)(2,1)}, f32[384,384]{1,0:T(8,128)}, f32[384,384]{1,0:T(8,128)}, f32[1,1152]{1,0:T(1,128)}) custom-call(bf16[256,1152]{1,0:T(8,128)(2,1)} %bitcast.76, f32[224,1152]{1,0:T(8,128)} %get-tuple-element.32.spectrum, f32[224,1152]{1,0:T(8,128)} %get-tuple-element.33.pre_modes, ...), custom_call_target="tpu_custom_call" | custom-call | tf_op jit(solution)/shard_map/spectral_back/pallas_call | solution.py:574
  337.6 2.0 reshape.153
  342.8 32.7 %all-to-all-done.12 = bf16[8,2,384,384]{3,2,1,0:T(8,128)(2,1)} async-done(((bf16[8,2,384,384]{3,2,1,0:T(8,128)(2,1)}), bf16[8,2,384,384]{3,2,1,0:T(8,128)(2,1)}, u32[]{:S(2)}, u32[]{:S(2)}) %all-to-all-start.12) | async-done | bytes 4718624 | tf_op jit(solution)/shard_map/weight_grads/all_to_all | solution.py:629
  375.5 4.6 all-to-all-start.10
  380.1 4.0 reduce_sum.64
  384.1 10.7 %all-to-all-done.10 = f32[32,10,128]{2,1,0:T(8,128)S(1)} async-done(((f32[32,10,128]{2,1,0:T(8,128)}), f32[32,10,128]{2,1,0:T(8,128)S(1)}, u32[]{:S(2)}, u32[]{:S(2)}) %all-to-all-start.10) | async-done | bytes 163872 | tf_op jit(solution)/shard_map/small_grads/all_to_all | solution.py:618
  394.8 3.6 all-to-all-start.13
  398.4 17.8 %all-to-all-done.13 = bf16[16,48,384]{2,1,0:T(8,128)(2,1)S(1)} async-done(((bf16[16,48,384]{2,1,0:T(8,128)(2,1)}), bf16[16,48,384]{2,1,0:T(8,128)(2,1)S(1)}, u32[]{:S(2)}, u32[]{:S(2)}) %all-to-all-start.13) | async-done | bytes 589856 | tf_op jit(solution)/shard_map/weight_grads/all_to_all | solution.py:631
  417.0 5.0 all-to-all-start.11
  422.1 14.6 %all-to-all-done.11 = f32[32,10,128]{2,1,0:T(8,128)S(1)} async-done(((f32[32,10,128]{2,1,0:T(8,128)}), f32[32,10,128]{2,1,0:T(8,128)S(1)}, u32[]{:S(2)}, u32[]{:S(2)}) %all-to-all-start.11) | async-done | bytes 163872 | tf_op jit(solution)/shard_map/small_grads/all_to_all | solution.py:423
  436.7 22.8 %all_to_all.100 = bf16[16,48,384]{2,1,0:T(8,128)(2,1)S(1)} all-to-all(bf16[16,48,384]{2,1,0:T(8,128)(2,1)S(1)} %broadcast_in_dim.58), channel_id=1, replica_groups={{0,16,32,48,64,80,96,112,128,144,160,176,192,208,224,240},{8,24,40,56,7..., dimensions={0} | all-to-all | bytes 1179648 | tf_op jit(solution)/shard_map/weight_grads/all_to_all | solution.py:423
  459.5 3.9 all-to-all-start.8
  463.4 2.8 output.1
  468.0 16.6 %all-to-all-done.8 = bf16[32,8,1152]{2,1,0:T(8,128)(2,1)S(1)} async-done(((bf16[32,8,1152]{2,1,0:T(8,128)(2,1)}), bf16[32,8,1152]{2,1,0:T(8,128)(2,1)S(1)}, u32[]{:S(2)}, u32[]{:S(2)}) %all-to-all-start.8) | async-done | bytes 589856 | tf_op jit(solution)/shard_map/spectral_back/all_to_all | solution.py:589
  485.4 4.1 unmix.2
  489.5 1.4 broadcast_in_dim.56
  490.9 5.1 all-to-all-start.9
  496.6 4.7 all-to-all-done.9.back_stats
  502.0 2.8 unmix.3
  505.1 1.1 pad_maximum_fusion.1
  506.2 1.1 pad_maximum_fusion
  (95 shorter events, 18.3 us)
Async XLA Ops:
  7.2 108.2 %all-gather.3.cloned.1.call-start = ((), (), s32[]{:S(2)}) async-start(), calls=%async_computation.15 | async-start | bytes 5308416 | tf_op jit(solution)/shard_map/weights/all_gather | solution.py:445
  8.4 107.0 %copy-start.15 = (f32[96]{0:T(128)S(1)}, f32[96]{0:T(128)}, u32[]{:S(2)}) copy-start(f32[96]{0:T(128)} %param.21) | copy-start | bytes 1156
  8.4 107.0 %copy-start = (bf16[96,7,384]{2,0,1:T(8,128)(2,1)S(1)}, bf16[96,7,384]{2,0,1:T(8,128)(2,1)}, u32[]{:S(2)}) copy-start(bf16[96,7,384]{2,0,1:T(8,128)(2,1)} %param.17) | copy-start | bytes 1548292
  9.3 112.6 %copy-start.12 = (f32[2,1,96,96]{3,2,1,0:T(8,128)S(1)}, f32[2,1,96,96]{3,2,1,0:T(8,128)}, u32[]{:S(2)}) copy-start(f32[2,1,96,96]{3,2,1,0:T(8,128)} %param.20) | copy-start | bytes 221188
  9.3 112.8 %copy-start.13 = (f32[2,1,96,96]{3,2,1,0:T(8,128)S(1)}, f32[2,1,96,96]{3,2,1,0:T(8,128)}, u32[]{:S(2)}) copy-start(f32[2,1,96,96]{3,2,1,0:T(8,128)} %param.19) | copy-start | bytes 221188
  115.4 116.1 %collective-permute-start = (bf16[8,2,384,384]{3,2,1,0:T(8,128)(2,1)}, bf16[8,2,384,384]{3,2,1,0:T(8,128)(2,1)}, u32[]{:S(2)}, u32[]{:S(2)}) collective-permute-start(bf16[8,2,384,384]{3,2,1,0:T(8,128)(2,1)} %bitcast.73), channel_id=1, source_target_pairs={{0,8},{8,0},{16,24},{24,16},{32,40},{40,32},{48,56},{56,48},{64,72... | collective-permute-start | bytes 14155784 | tf_op jit(solution)/shard_map/weights/ppermute | solution.py:446
  115.4 6.9 %copy-start.14 = (f32[96]{0:T(128)S(1)}, f32[96]{0:T(128)}, u32[]{:S(2)}) copy-start(f32[96]{0:T(128)} %param.18) | copy-start | bytes 1156
  116.4 11.8 %all-to-all-start = ((f32[8,24,384]{2,1,0:T(8,128)}), f32[8,24,384]{2,1,0:T(8,128)S(1)}, u32[]{:S(2)}, u32[]{:S(2)}) async-start(f32[8,24,384]{2,1,0:T(8,128)} %broadcast_in_dim.52), calls=%async_computation | async-start | bytes 589824 | tf_op jit(solution)/shard_map/stats/all_to_all | solution.py:423
  133.1 30.9 %all-to-all-start.1 = ((bf16[32,8,1152]{2,1,0:T(8,128)(2,1)}), bf16[32,8,1152]{2,1,0:T(8,128)(2,1)S(1)}, u32[]{:S(2)}, u32[]{:S(2)}) async-start(bf16[32,8,1152]{2,1,0:T(8,128)(2,1)} %bitcast.78), calls=%async_computation.1 | async-start | bytes 1179648 | tf_op jit(solution)/shard_map/lon/all_to_all | solution.py:472
  143.2 3.6 copy-start.2
  143.2 3.6 copy-start.3
  163.9 0.8 copy-start.4
  175.4 25.1 %all-to-all-start.2 = ((bf16[32,8,1152]{2,1,0:T(8,128)(2,1)}), bf16[32,8,1152]{2,1,0:T(8,128)(2,1)S(1)}, u32[]{:S(2)}, u32[]{:S(2)}) async-start(bf16[32,8,1152]{2,1,0:T(8,128)(2,1)} %bitcast.83), calls=%async_computation.2 | async-start | bytes 1179648 | tf_op jit(solution)/shard_map/spectral/all_to_all | solution.py:511
  200.5 5.4 %copy-start.7 = (bf16[32,8,1152]{2,1,0:T(8,128)(2,1)}, bf16[32,8,1152]{2,1,0:T(8,128)(2,1)S(1)}, u32[]{:S(2)}) copy-start(bf16[32,8,1152]{2,1,0:T(8,128)(2,1)S(1)} %all-to-all-done.2) | copy-start | bytes 1769476
  200.5 12.9 %all-to-all-start.4 = ((bf16[8,56,576]{2,1,0:T(8,128)(2,1)}), bf16[8,56,576]{2,1,0:T(8,128)(2,1)S(1)}, u32[]{:S(2)}, u32[]{:S(2)}) async-start(bf16[8,56,576]{2,1,0:T(8,128)(2,1)} %cot.1), calls=%async_computation.4 | async-start | bytes 1146880 | tf_op jit(solution)/shard_map/cot/all_to_all | solution.py:476
  213.4 18.1 %copy-start.9 = (bf16[8,56,576]{2,1,0:T(8,128)(2,1)}, bf16[8,56,576]{2,1,0:T(8,128)(2,1)S(1)}, u32[]{:S(2)}) copy-start(bf16[8,56,576]{2,1,0:T(8,128)(2,1)S(1)} %all-to-all-done.4.cot) | copy-start | bytes 1548292
  213.4 18.0 %all-to-all-start.3 = ((f32[8,56,576]{2,1,0:T(8,128)}), f32[8,56,576]{2,1,0:T(8,128)S(1)}, u32[]{:S(2)}, u32[]{:S(2)}) async-start(f32[8,56,576]{2,1,0:T(8,128)} %get-tuple-element.27), calls=%async_computation.3 | async-start | bytes 2293760 | tf_op jit(solution)/shard_map/mix/all_to_all | solution.py:520
  231.5 1.0 copy-start.1
  257.1 37.6 %collective-permute-start.1 = (bf16[8,2,384,384]{3,2,1,0:T(8,128)(2,1)}, bf16[8,2,384,384]{3,2,1,0:T(8,128)(2,1)}, u32[]{:S(2)}, u32[]{:S(2)}) collective-permute-start(bf16[8,2,384,384]{3,2,1,0:T(8,128)(2,1)} %get-tuple-element.43), channel_id=1, source_target_pairs={{0,8},{8,0},{16,24},{24,16},{32,40},{40,32},{48,56},{56,48},{64,72... | collective-permute-start | bytes 14155784 | tf_op jit(solution)/shard_map/weight_grads/ppermute | solution.py:627
  274.4 13.7 %all-to-all-start.5 = ((bf16[8,56,576]{2,1,0:T(8,128)(2,1)}), bf16[8,56,576]{2,1,0:T(8,128)(2,1)S(1)}, u32[]{:S(2)}, u32[]{:S(2)}) async-start(bf16[8,56,576]{2,1,0:T(8,128)(2,1)} %get-tuple-element.28), calls=%async_computation.5 | async-start | bytes 1146880 | tf_op jit(solution)/shard_map/output/all_to_all | solution.py:570
  288.1 15.1 %copy-start.8 = (bf16[8,56,576]{2,1,0:T(8,128)(2,1)}, bf16[8,56,576]{2,1,0:T(8,128)(2,1)S(1)}, u32[]{:S(2)}) copy-start(bf16[8,56,576]{2,1,0:T(8,128)(2,1)S(1)} %all-to-all-done.5.chunks) | copy-start | bytes 1548292
  288.1 27.7 %all-to-all-start.7 = ((bf16[32,8,1152]{2,1,0:T(8,128)(2,1)}), bf16[32,8,1152]{2,1,0:T(8,128)(2,1)S(1)}, u32[]{:S(2)}, u32[]{:S(2)}) async-start(bf16[32,8,1152]{2,1,0:T(8,128)(2,1)} %bitcast.82), calls=%async_computation.7 | async-start | bytes 1179648 | tf_op jit(solution)/shard_map/lon_back/all_to_all | solution.py:567
  315.7 0.8 copy-start.5
  316.6 58.9 %all-to-all-start.12 = ((bf16[8,2,384,384]{3,2,1,0:T(8,128)(2,1)}), bf16[8,2,384,384]{3,2,1,0:T(8,128)(2,1)}, u32[]{:S(2)}, u32[]{:S(2)}) async-start(bf16[8,2,384,384]{3,2,1,0:T(8,128)(2,1)} %add_convert_fusion), calls=%async_computation.12 | async-start | bytes 9437184 | tf_op jit(solution)/shard_map/weight_grads/all_to_all | solution.py:629
  337.6 2.4 copy-start.11
  375.5 19.3 %all-to-all-start.10 = ((f32[32,10,128]{2,1,0:T(8,128)}), f32[32,10,128]{2,1,0:T(8,128)S(1)}, u32[]{:S(2)}, u32[]{:S(2)}) async-start(f32[32,10,128]{2,1,0:T(8,128)} %reshape.156), calls=%async_computation.10 | async-start | bytes 524288 | tf_op jit(solution)/shard_map/small_grads/all_to_all | solution.py:618
  394.8 21.5 %all-to-all-start.13 = ((bf16[16,48,384]{2,1,0:T(8,128)(2,1)}), bf16[16,48,384]{2,1,0:T(8,128)(2,1)S(1)}, u32[]{:S(2)}, u32[]{:S(2)}) async-start(bf16[16,48,384]{2,1,0:T(8,128)(2,1)} %bitcast.37), calls=%async_computation.13 | async-start | bytes 1179648 | tf_op jit(solution)/shard_map/weight_grads/all_to_all | solution.py:631
  417.0 19.7 %all-to-all-start.11 = ((f32[32,10,128]{2,1,0:T(8,128)}), f32[32,10,128]{2,1,0:T(8,128)S(1)}, u32[]{:S(2)}, u32[]{:S(2)}) async-start(f32[32,10,128]{2,1,0:T(8,128)} %broadcast_in_dim.57), calls=%async_computation.11 | async-start | bytes 524288 | tf_op jit(solution)/shard_map/small_grads/all_to_all | solution.py:423
  459.5 25.1 %all-to-all-start.8 = ((bf16[32,8,1152]{2,1,0:T(8,128)(2,1)}), bf16[32,8,1152]{2,1,0:T(8,128)(2,1)S(1)}, u32[]{:S(2)}, u32[]{:S(2)}) async-start(bf16[32,8,1152]{2,1,0:T(8,128)(2,1)} %bitcast.26), calls=%async_computation.8 | async-start | bytes 1179648 | tf_op jit(solution)/shard_map/spectral_back/all_to_all | solution.py:589
  466.3 38.5 %collective-permute-start.2 = (bf16[2,384,384]{2,1,0:T(8,128)(2,1)S(1)}, bf16[2,384,384]{2,1,0:T(8,128)(2,1)S(1)}, u32[]{:S(2)}, u32[]{:S(2)}) collective-permute-start(bf16[2,384,384]{2,1,0:T(8,128)(2,1)S(1)} %bitcast.80), channel_id=1, source_target_pairs={{0,8},{8,0},{16,24},{24,16},{32,40},{40,32},{48,56},{56,48},{64,72... | collective-permute-start | bytes 1769480 | tf_op jit(solution)/shard_map/weight_grads/ppermute | solution.py:635
  484.6 0.8 copy-start.6
  490.9 10.4 %all-to-all-start.9 = ((f32[8,16,384]{2,1,0:T(8,128)}), f32[8,16,384]{2,1,0:T(8,128)S(1)}, u32[]{:S(2)}, u32[]{:S(2)}) async-start(f32[8,16,384]{2,1,0:T(8,128)} %broadcast_in_dim.56), calls=%async_computation.9 | async-start | bytes 393216 | tf_op jit(solution)/shard_map/unmix/all_to_all | solution.py:423
  501.3 0.7 copy-start.10
Sparse Core Ops, SparseCore 0:
  10.4 104.9 all-gather.2
